TPU v7x, 512 devices: a whole 4x8x8 slice. The times are simulated.
512 devices in a mesh: row: 16 (over y, x_hi), col: 32 (over x_lo, z, core).
Axes of the slice: x: 4 (x_hi: 2, x_lo: 2; x = x_hi * 2 + x_lo), y: 8, z: 8, core: 2. Of those that a mesh axis runs over, the one named last changes fastest.
Arguments:
- height: float32 [2048, 4096], P('row', 'col'), may hold values from -6 to 6
- density: float32 [2048, 4096], P('row', 'col'), may hold values from 0.2 to 1
- target: float32 [2048, 4096], P('row', 'col'), may hold values from -6 to 6
- region_of_block: int32 [16, 32], P('row', 'col'), may hold values from 0 to 127
- class_of_block: int32 [16, 32], P('row', 'col'), may hold values from 0 to 7
- fill_level: float32 [128], replicated, may hold values from 0 to 0.5
- rates: float32 [8], replicated, may hold values from 0.1 to 0.6
- col_taps: float32 [8, 33], replicated, may hold values from -1 to 1
- row_taps: float32 [8, 33], replicated, may hold values from -1 to 1
- gains: float32 [8], replicated, may hold values from 0.2 to 0.6
Outputs:
- new_height: float32 [2048, 4096], P('row', 'col')
- gain_grad: float32 [8], replicated
- fill_grad: float32 [128], replicated
All inputs are finite; a program needn't handle non-finite values.
Results may differ from a plain program's by a relative error of at most 0.00035.
The roundings to bfloat16 on the way count: a program that leaves them out, or rounds other values in their place, can miss the bound.
Values may be sent and summed in bfloat16 or wider, within the bound.
No kernel may reach another device: no remote copies, remote signals or barrier semaphores. Data moves between devices by JAX's collectives and lax.ppermute only.
A program may use at most 128 MiB of HBM per device.

v0:
```python
import jax
import jax.numpy as jnp
from jax import lax
from jax.sharding import PartitionSpec as P

CHANNELS = 8
TAPS = 33
BLOCK = 128


def kernel_table(tap_weights, length):
    table = []
    for channel in range(CHANNELS):
        grouped = {}
        ordered = []
        for position in range(TAPS):
            offset = (position - TAPS // 2) * 2**channel % length
            if offset not in grouped:
                grouped[offset] = []
                ordered.append(offset)
            grouped[offset].append(position)
        entries = []
        for offset in ordered:
            summed = jnp.zeros((), jnp.float32)
            for position in grouped[offset]:
                summed = summed + tap_weights[channel, position]
            rounded = lax.optimization_barrier(summed.astype(jnp.bfloat16)).astype(jnp.float32)
            entries.append((offset, rounded))
        table.append(entries)
    return table


def shift_sum(band, entries, first, local_len, axis, direction):
    total = band.shape[axis]
    doubled = jnp.concatenate([band, band], axis=axis)
    summed = None
    for offset, weight in entries:
        start = jnp.mod(first + direction * offset, total)
        window = lax.dynamic_slice_in_dim(doubled, start, local_len, axis)
        term = weight * window.astype(jnp.float32)
        summed = term if summed is None else summed + term
    return summed


def spread_add(placed_terms, template_shape, total, axis):
    local_len = template_shape[axis]
    wide_shape = list(template_shape)
    wide_shape[axis] = total + local_len
    running = jnp.zeros(tuple(wide_shape), jnp.float32)
    for start, contribution in placed_terms:
        window = lax.dynamic_slice_in_dim(running, start, local_len, axis)
        running = lax.dynamic_update_slice_in_dim(running, window + contribution, start, axis)
    head = lax.slice_in_dim(running, 0, local_len, axis=axis) + lax.slice_in_dim(
        running, total, total + local_len, axis=axis
    )
    middle = lax.slice_in_dim(running, local_len, total, axis=axis)
    return jnp.concatenate([head, middle], axis=axis)


def shards(
    height,
    density,
    target,
    region_of_block,
    class_of_block,
    fill_level,
    rates,
    col_taps,
    row_taps,
    gains,
):
    rows_here, cols_here = height.shape
    total_rows = rows_here * lax.axis_size("row")
    total_cols = cols_here * lax.axis_size("col")
    row_first = lax.axis_index("row") * rows_here
    col_first = lax.axis_index("col") * cols_here
    block_rows, block_cols = region_of_block.shape
    block_side = rows_here // block_rows
    region_hot = (
        region_of_block[:, :, None] == jnp.arange(fill_level.shape[0], dtype=jnp.int32)
    ).astype(jnp.float32)
    class_hot = (class_of_block[:, :, None] == jnp.arange(rates.shape[0], dtype=jnp.int32)).astype(
        jnp.float32
    )
    fill_block = jnp.sum(region_hot * fill_level, axis=2)
    rate_block = jnp.sum(class_hot * rates, axis=2)

    def to_cells(values):
        spread_out = jnp.broadcast_to(
            values[:, None, :, None], (block_rows, block_side, block_cols, block_side)
        )
        return spread_out.reshape(rows_here, cols_here)

    effective = density + to_cells(fill_block)
    rate_cells = to_cells(rate_block)
    source = (effective * height).astype(jnp.bfloat16)
    col_table = kernel_table(col_taps, total_cols)
    row_table = kernel_table(row_taps, total_rows)
    source_band = lax.all_gather(source, "col", axis=1, tiled=True)
    smoothed = jnp.stack(
        [
            shift_sum(source_band, col_table[channel], col_first, cols_here, 1, -1)
            for channel in range(CHANNELS)
        ]
    ).astype(jnp.bfloat16)
    channel_band = lax.all_gather(smoothed, "row", axis=1, tiled=True)
    pressure_arg = jnp.zeros((rows_here, cols_here), jnp.float32)
    for channel in range(CHANNELS):
        pressure_arg = pressure_arg + gains[channel] * shift_sum(
            channel_band[channel], row_table[channel], row_first, rows_here, 0, -1
        )
    shifted = 1.0 + pressure_arg
    new_height = height - rate_cells * jax.nn.softplus(shifted)
    pressure_adjoint = (
        -(new_height - target) * rate_cells * jax.nn.sigmoid(shifted) / BLOCK
    ).astype(jnp.bfloat16)
    adjoint_band = lax.all_gather(pressure_adjoint, "row", axis=0, tiled=True)
    channel_adjoint = jnp.stack(
        [
            shift_sum(adjoint_band, row_table[channel], row_first, rows_here, 0, 1)
            for channel in range(CHANNELS)
        ]
    )
    gain_local = jnp.sum(channel_adjoint * smoothed.astype(jnp.float32), axis=(1, 2))
    gain_grad = lax.psum(gain_local, ("row", "col"))
    weighted = (gains[:, None, None] * channel_adjoint).astype(jnp.bfloat16)
    placed_columns = []
    for channel in range(CHANNELS):
        channel_values = weighted[channel].astype(jnp.float32)
        for offset, weight in col_table[channel]:
            start = jnp.mod(col_first - offset, total_cols)
            placed_columns.append((start, weight * channel_values))
    column_terms = spread_add(placed_columns, (rows_here, cols_here), total_cols, 1)
    source_adjoint = lax.psum_scatter(
        column_terms.astype(jnp.bfloat16), "col", scatter_dimension=1, tiled=True
    ).astype(jnp.float32)
    block_sums = jnp.sum(
        (source_adjoint * height).reshape(block_rows, block_side, block_cols, block_side),
        axis=(1, 3),
    )
    fill_local = jnp.sum(region_hot * block_sums[:, :, None], axis=(0, 1))
    fill_grad = lax.psum(fill_local, ("row", "col"))
    return (new_height, gain_grad, fill_grad)


def solution(mesh):
    in_specs = (
        P("row", "col"),
        P("row", "col"),
        P("row", "col"),
        P("row", "col"),
        P("row", "col"),
        P(),
        P(),
        P(),
        P(),
        P(),
    )
    out_specs = (P("row", "col"), P(), P())
    return jax.shard_map(shards, mesh=mesh, in_specs=in_specs, out_specs=out_specs, check_vma=False)
```

profile of v0, /device:TPU:1, one launch (start us, length us, event | category | flops | bytes accessed | tf_op | source)
XLA Modules:
  0.0 1034.6 jit_solution(17635049522354549897)
XLA Ops:
  7.9 1.3 fusion.1270
  9.1 2.1 multiply_convert_fusion.2
  191.6 1.4 constant_dynamic-update-slice_fusion.1
  194.0 1.0 constant_dynamic-update-slice_fusion.8
  195.0 1.0 constant_dynamic-update-slice_fusion.7
  196.0 1.0 constant_dynamic-update-slice_fusion.6
  197.0 1.0 constant_dynamic-update-slice_fusion.5
  198.0 1.0 constant_dynamic-update-slice_fusion.4
  198.9 1.3 constant_dynamic-update-slice_fusion.3
  200.3 1.0 constant_dynamic-update-slice_fusion.2
  387.4 2.4 slice_bitcast_fusion.4
  393.0 1.0 fusion.1073
  405.0 1.3 fusion.1118
  411.0 89.8 %multiply_add_fusion.1 = f32[128,128]{1,0:T(8,128)S(1)} fusion(s32[]{:T(128)S(6)} %select_n.5624, bf16[2048,128]{1,0:T(8,128)(2,1)S(1)} %get-tuple-element.12, s32[]{:T(128)S(6)} %select_n.5594, s32[]{:T(128)S(6)} %select_n.5596, s32[]{:T(128)S(6)} %select_n.5598, s32[]{:T(128)S(6)} %select_n.5600, s32[]{:T(128)S(6)} %select_n.5602, s32[]{:T(128)S(6)} %select_n.5604, ...), kind=kLoop, calls=%fused_computation.2697 | loop fusion | flops 9764864 | bytes 2687446 | tf_op jit(solution)/shard_map/add | solution.py:109
  500.8 16.8 %multiply_convert_fusion.1 = (bf16[128,128]{1,0:T(8,128)(2,1)S(1)}, f32[128,128]{1,0:T(8,128)}) fusion(f32[128,128]{1,0:T(8,128)S(1)} %copy-done.5, f32[]{:T(128)} %fusion.1271, f32[128,128]{1,0:T(8,128)S(1)} %copy-done.3, bf16[128,128]{1,0:T(8,128)(2,1)S(1)} %get-tuple-element.171, f32[]{:T(128)S(6)} %convert_element_type.6866, ...), kind=kLoop, calls=%fused_computation.2693 | loop fusion | flops 8699904 | bytes 4915900 | tf_op jit(solution)/shard_map/convert_element_type | solution.py:116
  517.6 38.2 %all_gather.11 = bf16[2048,128]{1,0:T(8,128)(2,1)S(1)} all-gather(bf16[128,128]{1,0:T(8,128)(2,1)S(1)} %get-tuple-element.5), channel_id=1, replica_groups=mesh['row'=16,'col'=32] {'row'}, dimensions={0}, use_global_device_ids=true | all-gather | bytes 557056 | tf_op jit(solution)/shard_map/all_gather | solution.py:117
  557.6 1.0 bitcast_dynamic-update-slice_fusion.4
  562.9 1.0 dynamic_update_slice.789
  594.1 1.1 dynamic_update_slice.822
  625.4 1.2 dynamic_update_slice.855
  718.3 1.1 dynamic_update_slice.954
  801.4 1.3 copy.13
  802.7 123.6 %reduce-scatter.4.cloned.1.call-done = bf16[128,128]{1,0:T(8,128)(2,1)} async-done(((bf16[4096,128]{1,0:T(8,128)(2,1)}), bf16[128,128]{1,0:T(8,128)(2,1)}) %reduce-scatter.4.cloned.1.call-update) | async-done | bytes 32784
  928.5 99.2 %all-reduce = (f32[8]{0:T(128)}, f32[128]{0:T(128)}) all-reduce(f32[8]{0:T(128)S(1)} %get-tuple-element.16, f32[128]{0:T(128)S(1)} %compare_select_fusion.2), channel_id=1, replica_groups=mesh['row'=16,'col'=32] {'row','col'}, use_global_device_ids=true, to_apply=%region_3.4 | all-reduce | flops 136 | bytes 1088 | tf_op jit(solution)/shard_map/psum | solution.py:125
  (626 shorter events, 282.4 us)
Async XLA Ops:
  7.2 6.6 copy-start.7
  7.2 184.4 %all-gather.3.cloned.1.call-start = ((), (), s32[]{:S(2)}) async-start(), calls=%async_computation.1 | async-start | bytes 1081344 | tf_op jit(solution)/shard_map/all_gather | solution.py:99
  11.3 376.1 %all-gather.5.cloned.1.call-start = ((), (), s32[]{:S(2)}) async-start(), calls=%async_computation.2 | async-start | bytes 4456448 | tf_op jit(solution)/shard_map/all_gather | solution.py:106
  191.6 1.5 copy-start
  201.2 0.7 copy-start.1
  202.0 724.3 %reduce-scatter.4.cloned.1.call-start = ((), (), s32[]{:S(2)}) async-start(), calls=%async_computation.3 | async-start | bytes 1081344
  203.8 1.9 copy-start.4
  205.1 181.0 %copy-start.8 = (f32[8]{0:T(128)S(1)}, f32[8]{0:T(128)}, u32[]{:S(2)}) copy-start(f32[8]{0:T(128)} %param.16) | copy-start | bytes 100
  205.1 181.6 %copy-start.6 = (f32[8]{0:T(128)S(1)}, f32[8]{0:T(128)}, u32[]{:S(2)}) copy-start(f32[8]{0:T(128)} %param.19) | copy-start | bytes 100
  410.2 90.5 %copy-start.3 = (f32[128,128]{1,0:T(8,128)S(1)}, f32[128,128]{1,0:T(8,128)}, u32[]{:S(2)}) copy-start(f32[128,128]{1,0:T(8,128)} %param.10) | copy-start | bytes 196612
  410.2 90.5 %copy-start.5 = (f32[128,128]{1,0:T(8,128)S(1)}, f32[128,128]{1,0:T(8,128)}, u32[]{:S(2)}) copy-start(f32[128,128]{1,0:T(8,128)} %param.12) | copy-start | bytes 196612
  559.5 3.0 copy-start.2
Sparse Core Ops, SparseCore 0:
  11.4 71.6 all-gather.2
  202.1 107.3 all-gather.4
  802.8 123.4 reduce-scatter.3
where the time goes:
time: 1050 us; the launch traced here: 1030 us
  between operations  361 us (34%)
  local copies, waits for them, and re-layouts  242 us (23%)
  other arithmetic  170 us (16%)
  blocking collectives  137 us (13%)
  waiting for transfers between devices  124 us (12%)
    dynamic_update_slice x263, local copies, waits for them, and re-layouts, spread_add(): lax.dynamic_update_slice_in_dim(running, window + contribution, start, axis)  210 us
    unnamed x4, waiting for transfers between devices  124 us
    psum x1, blocking collectives, shards(): gain_grad = lax.psum(gain_local, ('row', 'col'))  99.2 us
    add x1, other arithmetic, shards(): pressure_arg + gains[channel] * shift_sum(channel_band[channel], row_tabl...  89.8 us
    all_gather x1, blocking collectives, shards(): adjoint_band = lax.all_gather(pressure_adjoint, 'row', axis=0, tiled=True)  38.2 us
    add x262, other arithmetic, spread_add(): window + contribution  24.3 us
    slice x31, local copies, waits for them, and re-layouts, kernel_table(): summed = summed + tap_weights[channel, position]  22.2 us
  transfers between devices with their start and end apart: 3, of which 1 were waited for; matrix products, arithmetic and copies ran while one was open for 2% of the time, Pallas kernels for 0%

commit v1 on v0

--- a/solution.py
+++ b/solution.py
@@ -122,7 +122,9 @@
         ]
     )
     gain_local = jnp.sum(channel_adjoint * smoothed.astype(jnp.float32), axis=(1, 2))
-    gain_grad = lax.psum(gain_local, ("row", "col"))
+    gain_grad = gain_local
+    for name in ("col", "row"):
+        gain_grad = lax.psum(gain_grad, name)
     weighted = (gains[:, None, None] * channel_adjoint).astype(jnp.bfloat16)
     placed_columns = []
     for channel in range(CHANNELS):

time: 1050 us -> 1050 us (level)
  blocking collectives: 137 us -> 234 us
  waiting for transfers between devices: 124 us -> 28.3 us
    psum x1 -> x3, blocking collectives: 99.2 us -> 196 us  [the longest x1 99.7 us: shards(): fill_grad = lax.psum(fill_local, ('row', 'col'))]
    unnamed x4, waiting for transfers between devices: 124 us -> 28.2 us
where the time goes in v1:
time: 1050 us; the launch traced here: 1030 us
  between operations  360 us (34%)
  local copies, waits for them, and re-layouts  242 us (23%)
  blocking collectives  234 us (22%)
  other arithmetic  170 us (16%)
  waiting for transfers between devices  28.3 us (3%)
    dynamic_update_slice x263, local copies, waits for them, and re-layouts, spread_add(): lax.dynamic_update_slice_in_dim(running, window + contribution, start, axis)  210 us
    psum x1, blocking collectives, shards(): fill_grad = lax.psum(fill_local, ('row', 'col'))  99.7 us
    psum x2, blocking collectives, shards(): gain_grad = lax.psum(gain_grad, name)  95.8 us
    add x1, other arithmetic, shards(): pressure_arg + gains[channel] * shift_sum(channel_band[channel], row_tabl...  89.8 us
    all_gather x1, blocking collectives, shards(): adjoint_band = lax.all_gather(pressure_adjoint, 'row', axis=0, tiled=True)  38.1 us
    unnamed x4, waiting for transfers between devices  28.2 us
    add x262, other arithmetic, spread_add(): window + contribution  24.3 us
    slice x31, local copies, waits for them, and re-layouts, kernel_table(): summed = summed + tap_weights[channel, position]  22.2 us
  transfers between devices with their start and end apart: 3, of which 1 were waited for; matrix products, arithmetic and copies ran while one was open for 2% of the time, Pallas kernels for 0%

profile of v1, /device:TPU:1, one launch (start us, length us, event | category | flops | bytes accessed | tf_op | source)
XLA Modules:
  0.0 1033.9 jit_solution(12319519080617623031)
XLA Ops:
  7.9 1.3 fusion.1270
  9.1 2.1 multiply_convert_fusion.2
  190.6 1.4 constant_dynamic-update-slice_fusion.1
  193.0 1.0 constant_dynamic-update-slice_fusion.8
  194.0 1.0 constant_dynamic-update-slice_fusion.7
  195.0 1.0 constant_dynamic-update-slice_fusion.6
  195.9 1.0 constant_dynamic-update-slice_fusion.5
  196.9 1.0 constant_dynamic-update-slice_fusion.4
  197.9 1.3 constant_dynamic-update-slice_fusion.3
  386.0 2.4 slice_bitcast_fusion.4
  391.6 1.0 fusion.1073
  403.6 1.3 fusion.1118
  409.6 89.8 %multiply_add_fusion.1 = f32[128,128]{1,0:T(8,128)S(1)} fusion(s32[]{:T(128)S(6)} %select_n.5624, bf16[2048,128]{1,0:T(8,128)(2,1)S(1)} %get-tuple-element.10, s32[]{:T(128)S(6)} %select_n.5594, s32[]{:T(128)S(6)} %select_n.5596, s32[]{:T(128)S(6)} %select_n.5598, s32[]{:T(128)S(6)} %select_n.5600, s32[]{:T(128)S(6)} %select_n.5602, s32[]{:T(128)S(6)} %select_n.5604, ...), kind=kLoop, calls=%fused_computation.2697 | loop fusion | flops 9764864 | bytes 2687446 | tf_op jit(solution)/shard_map/add | solution.py:109
  499.5 16.6 %multiply_convert_fusion.1 = (bf16[128,128]{1,0:T(8,128)(2,1)S(1)}, f32[128,128]{1,0:T(8,128)}) fusion(f32[128,128]{1,0:T(8,128)S(1)} %copy-done.5, f32[]{:T(128)} %fusion.1271, f32[128,128]{1,0:T(8,128)S(1)} %copy-done.3, bf16[128,128]{1,0:T(8,128)(2,1)S(1)} %get-tuple-element.169, f32[]{:T(128)S(6)} %convert_element_type.6866, ...), kind=kLoop, calls=%fused_computation.2693 | loop fusion | flops 8699904 | bytes 4915900 | tf_op jit(solution)/shard_map/convert_element_type | solution.py:116
  516.1 38.1 %all_gather.11 = bf16[2048,128]{1,0:T(8,128)(2,1)S(1)} all-gather(bf16[128,128]{1,0:T(8,128)(2,1)S(1)} %get-tuple-element.3), channel_id=1, replica_groups=mesh['row'=16,'col'=32] {'row'}, dimensions={0}, use_global_device_ids=true | all-gather | bytes 557056 | tf_op jit(solution)/shard_map/all_gather | solution.py:117
  561.3 1.0 dynamic_update_slice.789
  592.5 1.1 dynamic_update_slice.822
  623.8 1.2 dynamic_update_slice.855
  716.7 1.1 dynamic_update_slice.954
  799.8 1.3 copy.13
  801.1 65.6 %psum.21 = f32[8]{0:T(128)S(1)} all-reduce(f32[8]{0:T(128)S(1)} %get-tuple-element.14), channel_id=1, replica_groups=mesh['row'=16,'col'=32] {'col'}, use_global_device_ids=true, to_apply=%region_3.4 | all-reduce | flops 8 | bytes 64 | tf_op jit(solution)/shard_map/psum | solution.py:127
  866.7 30.3 %psum.22 = f32[8]{0:T(128)} all-reduce(f32[8]{0:T(128)S(1)} %psum.21), channel_id=1, replica_groups=mesh['row'=16,'col'=32] {'row'}, use_global_device_ids=true, to_apply=%region_4.5 | all-reduce | flops 8 | bytes 64 | tf_op jit(solution)/shard_map/psum | solution.py:127
  896.9 28.2 %reduce-scatter.4.cloned.1.call-done = bf16[128,128]{1,0:T(8,128)(2,1)} async-done(((bf16[4096,128]{1,0:T(8,128)(2,1)}), bf16[128,128]{1,0:T(8,128)(2,1)}) %reduce-scatter.4.cloned.1.call-update) | async-done | bytes 32784
  927.3 99.7 %psum.23 = f32[128]{0:T(128)} all-reduce(f32[128]{0:T(128)S(1)} %compare_select_fusion.2), channel_id=1, replica_groups=mesh['row'=16,'col'=32] {'row','col'}, use_global_device_ids=true, to_apply=%region_7.8 | all-reduce | flops 128 | bytes 1024 | tf_op jit(solution)/shard_map/psum | solution.py:144
  (628 shorter events, 284.3 us)
Async XLA Ops:
  7.2 6.6 copy-start.7
  7.2 183.4 %all-gather.3.cloned.1.call-start = ((), (), s32[]{:S(2)}) async-start(), calls=%async_computation.1 | async-start | bytes 1081344 | tf_op jit(solution)/shard_map/all_gather | solution.py:99
  11.3 374.7 %all-gather.5.cloned.1.call-start = ((), (), s32[]{:S(2)}) async-start(), calls=%async_computation.2 | async-start | bytes 4456448 | tf_op jit(solution)/shard_map/all_gather | solution.py:106
  190.6 1.5 copy-start
  200.2 0.7 copy-start.1
  201.0 724.2 %reduce-scatter.4.cloned.1.call-start = ((), (), s32[]{:S(2)}) async-start(), calls=%async_computation.3 | async-start | bytes 1081344
  202.8 1.9 copy-start.4
  204.1 180.7 %copy-start.8 = (f32[8]{0:T(128)S(1)}, f32[8]{0:T(128)}, u32[]{:S(2)}) copy-start(f32[8]{0:T(128)} %param.16) | copy-start | bytes 100
  204.1 181.3 %copy-start.6 = (f32[8]{0:T(128)S(1)}, f32[8]{0:T(128)}, u32[]{:S(2)}) copy-start(f32[8]{0:T(128)} %param.19) | copy-start | bytes 100
  408.8 90.6 %copy-start.3 = (f32[128,128]{1,0:T(8,128)S(1)}, f32[128,128]{1,0:T(8,128)}, u32[]{:S(2)}) copy-start(f32[128,128]{1,0:T(8,128)} %param.10) | copy-start | bytes 196612
  408.8 90.6 %copy-start.5 = (f32[128,128]{1,0:T(8,128)S(1)}, f32[128,128]{1,0:T(8,128)}, u32[]{:S(2)}) copy-start(f32[128,128]{1,0:T(8,128)} %param.12) | copy-start | bytes 196612
  557.9 3.0 copy-start.2
Sparse Core Ops, SparseCore 0:
  11.4 71.6 all-gather.2
  201.1 107.4 all-gather.4
  801.2 123.8 reduce-scatter.3
